TPU v7x, 32 devices: a whole 2x2x4 slice. The times are simulated.
32 devices in a mesh: seq: 4 (over y, x), fsdp: 8 (over z, core).
Axes of the slice: x: 2, y: 2, z: 4, core: 2. Of those that a mesh axis runs over, the one named last changes fastest.
Arguments:
- tokens: bfloat16 [8, 1024, 2048], P('fsdp', 'seq'), may hold values from -6 to 6
- cotangent: bfloat16 [8, 1024, 2048], P('fsdp', 'seq'), may hold values from -6 to 6
- attn_gain: bfloat16 [2048], P('fsdp'), may hold values from 0.5 to 1.5
- attn_shift: bfloat16 [2048], P('fsdp'), may hold values from -1.25 to 1.25
- mlp_gain: bfloat16 [2048], P('fsdp'), may hold values from 0.5 to 1.5
- mlp_shift: bfloat16 [2048], P('fsdp'), may hold values from -1.25 to 1.25
- qkv_weight: bfloat16 [2048, 6144], P('fsdp'), may hold values from -0.375 to 0.375
- qkv_bias: bfloat16 [6144], P('fsdp'), may hold values from -1.25 to 1.25
- dense_weight: bfloat16 [2048, 2048], P('fsdp'), may hold values from -0.5 to 0.5
- dense_bias: bfloat16 [2048], P('fsdp'), may hold values from -1.25 to 1.25
- expand_weight: bfloat16 [2048, 8192], P(None, 'fsdp'), may hold values from -0.125 to 0.125
- expand_bias: bfloat16 [8192], P('fsdp'), may hold values from -1.25 to 1.25
- contract_weight: bfloat16 [8192, 2048], P('fsdp'), may hold values from -0.0625 to 0.0625
- contract_bias: bfloat16 [2048], P('fsdp'), may hold values from -1.25 to 1.25
Outputs:
- block_out: bfloat16 [8, 1024, 2048], P('fsdp', 'seq')
- input_grad: float32 [8, 1024, 2048], P('fsdp', 'seq')
- attngain_grad: float32 [2048], P('fsdp')
- attnshift_grad: float32 [2048], P('fsdp')
- mlpgain_grad: float32 [2048], P('fsdp')
- mlpshift_grad: float32 [2048], P('fsdp')
- qkvweight_grad: float32 [2048, 6144], P('fsdp')
- qkvbias_grad: float32 [6144], P('fsdp')
- denseweight_grad: float32 [2048, 2048], P('fsdp')
- densebias_grad: float32 [2048], P('fsdp')
- expandweight_grad: float32 [2048, 8192], P(None, 'fsdp')
- expandbias_grad: float32 [8192], P('fsdp')
- contractweight_grad: float32 [8192, 2048], P('fsdp')
- contractbias_grad: float32 [2048], P('fsdp')
All inputs are finite; a program needn't handle non-finite values.
Results may differ from a plain program's by a relative error of at most 0.0075.
The roundings to bfloat16 on the way count: a program that leaves them out, or rounds other values in their place, can miss the bound.
Values may be sent and summed in bfloat16 or wider, within the bound.
A program may use at most 384 MiB of HBM per device.

v0:
```python
from functools import partial

import jax
import jax.numpy as jnp
from jax import lax
from jax.sharding import PartitionSpec as P

HEADS = 8
HEAD_DIM = 256
ROT = 64


EPSILON = 1e-05


def layer_norm(values, ln_gain, ln_shift):
    center = jnp.mean(values, axis=-1, keepdims=True)
    offset_rows = values - center
    spread = jnp.mean(offset_rows * offset_rows, axis=-1, keepdims=True)
    return offset_rows * lax.rsqrt(spread + EPSILON) * ln_gain + ln_shift


def rotary_tables(positions):
    frequency = 1.0 / 10000.0 ** (jnp.arange(0, ROT, 2, dtype=jnp.float32) / ROT)
    angles = positions.astype(jnp.float32)[:, None] * frequency[None, :]
    return (jnp.cos(angles)[:, None, :], jnp.sin(angles)[:, None, :])


def rotate(head_rows, cosine, sine):
    half_rot = ROT // 2
    first_half = head_rows[..., :half_rot]
    second = head_rows[..., half_rot:ROT]
    return jnp.concatenate(
        [
            first_half * cosine - second * sine,
            second * cosine + first_half * sine,
            head_rows[..., ROT:],
        ],
        axis=-1,
    )


def dot_plain(left, right):
    return jnp.dot(left, right, preferred_element_type=jnp.float32)


def dot_right(left, right):
    return lax.dot_general(
        left, right, (((1,), (1,)), ((), ())), preferred_element_type=jnp.float32
    )


def dot_left(left, right):
    return lax.dot_general(
        left, right, (((0,), (0,)), ((), ())), preferred_element_type=jnp.float32
    )


def attend_forward(queries, key_rows, value_rows):
    length = queries.shape[0]
    block_size = min(512, length)
    score_scale = HEAD_DIM ** (-0.5)
    key_index = lax.iota(jnp.int32, length)
    outputs = []
    totals = []
    for offset in range(0, length, block_size):
        query_block = queries[offset : offset + block_size]
        scores = dot_right(query_block, key_rows) * score_scale
        causal = (offset + lax.iota(jnp.int32, block_size))[:, None] >= key_index[None, :]
        scores = jnp.where(causal, scores, -jnp.inf)
        largest = jnp.max(scores, axis=-1, keepdims=True)
        exponent = jnp.exp(scores - largest)
        row_total = jnp.sum(exponent, axis=-1, keepdims=True)
        attn_probs = (exponent / row_total).astype(jnp.bfloat16)
        outputs.append(dot_plain(attn_probs, value_rows))
        totals.append((largest + jnp.log(row_total))[:, 0])
    return (jnp.concatenate(outputs, axis=0), jnp.concatenate(totals, axis=0))


def attend_backward(queries, key_rows, value_rows, context_grad, log_total):
    length = queries.shape[0]
    block_size = min(512, length)
    score_scale = HEAD_DIM ** (-0.5)
    key_index = lax.iota(jnp.int32, length)
    query_grads = []
    key_grad = jnp.zeros((length, queries.shape[1]), jnp.float32)
    value_grad = jnp.zeros((length, queries.shape[1]), jnp.float32)
    for offset in range(0, length, block_size):
        query_block = queries[offset : offset + block_size]
        grad_block = context_grad[offset : offset + block_size]
        scores = dot_right(query_block, key_rows) * score_scale
        causal = (offset + lax.iota(jnp.int32, block_size))[:, None] >= key_index[None, :]
        scores = jnp.where(causal, scores, -jnp.inf)
        attn_probs = jnp.exp(scores - log_total[offset : offset + block_size, None])
        probs_low = attn_probs.astype(jnp.bfloat16)
        probs_grad = dot_right(grad_block, value_rows)
        inner_sum = jnp.sum(attn_probs * probs_grad, axis=-1, keepdims=True)
        score_grad = (attn_probs * (probs_grad - inner_sum)).astype(jnp.bfloat16)
        query_grads.append(dot_plain(score_grad, key_rows) * score_scale)
        key_grad = key_grad + dot_left(score_grad, query_block) * score_scale
        value_grad = value_grad + dot_left(probs_low, grad_block)
    return (jnp.concatenate(query_grads, axis=0), key_grad, value_grad)


def forward_item(triple):
    return attend_forward(triple[0], triple[1], triple[2])


def backward_item(packed):
    triple = packed[0]
    return attend_backward(triple[0], triple[1], triple[2], packed[1], packed[2])


def shards(
    tokens,
    cotangent,
    attn_gain,
    attn_shift,
    mlp_gain,
    mlp_shift,
    qkv_weight,
    qkv_bias,
    dense_weight,
    dense_bias,
    expand_weight,
    expand_bias,
    contract_weight,
    contract_bias,
):
    seq_count, local_len, feat_width = tokens.shape
    row_count = seq_count * local_len
    head_local = HEADS // lax.axis_size("seq")
    x_rows = tokens.reshape(row_count, feat_width).astype(jnp.float32)
    zero_shift = jnp.zeros((feat_width,), jnp.float32)
    (
        full_attngain,
        full_attnshift,
        full_mlpgain,
        full_mlpshift,
        full_qkv,
        full_qkvbias,
        full_dense,
        full_densebias,
        full_contractbias,
    ) = (
        lax.all_gather(attn_gain, "fsdp", axis=0, tiled=True),
        lax.all_gather(attn_shift, "fsdp", axis=0, tiled=True),
        lax.all_gather(mlp_gain, "fsdp", axis=0, tiled=True),
        lax.all_gather(mlp_shift, "fsdp", axis=0, tiled=True),
        lax.all_gather(qkv_weight, "fsdp", axis=0, tiled=True),
        lax.all_gather(qkv_bias, "fsdp", axis=0, tiled=True),
        lax.all_gather(dense_weight, "fsdp", axis=0, tiled=True),
        lax.all_gather(dense_bias, "fsdp", axis=0, tiled=True),
        lax.all_gather(contract_bias, "fsdp", axis=0, tiled=True),
    )
    attn_in = layer_norm(
        x_rows, full_attngain.astype(jnp.float32), full_attnshift.astype(jnp.float32)
    ).astype(jnp.bfloat16)
    projected = (dot_plain(attn_in, full_qkv) + full_qkvbias.astype(jnp.float32)).reshape(
        seq_count, local_len, 3, HEADS, HEAD_DIM
    )
    positions = lax.axis_index("seq") * local_len + lax.iota(jnp.int32, local_len)
    cosine_table, sine_table = rotary_tables(positions)
    outgoing = jnp.stack(
        [
            rotate(projected[:, :, 0], cosine_table, sine_table),
            rotate(projected[:, :, 1], cosine_table, sine_table),
            projected[:, :, 2],
        ],
        axis=2,
    ).astype(jnp.bfloat16)
    by_head = lax.all_to_all(outgoing, "seq", split_axis=3, concat_axis=1, tiled=True)
    full_len = by_head.shape[1]
    per_item = jnp.transpose(by_head, (0, 3, 2, 1, 4)).reshape(
        seq_count * head_local, 3, full_len, HEAD_DIM
    )
    attended, log_total = lax.map(forward_item, per_item)
    heads_out = jnp.transpose(
        attended.astype(jnp.bfloat16).reshape(seq_count, head_local, full_len, HEAD_DIM),
        (0, 2, 1, 3),
    )
    context = lax.all_to_all(heads_out, "seq", split_axis=1, concat_axis=2, tiled=True).reshape(
        row_count, feat_width
    )
    attn_out = dot_plain(context, full_dense) + full_densebias.astype(jnp.float32)
    mlp_in = layer_norm(
        x_rows, full_mlpgain.astype(jnp.float32), full_mlpshift.astype(jnp.float32)
    ).astype(jnp.bfloat16)
    group_rows = lax.all_gather(mlp_in, "fsdp", axis=0, tiled=True)
    pre_act = dot_plain(group_rows, expand_weight) + expand_bias.astype(jnp.float32)
    act_low = jax.nn.gelu(pre_act, approximate=False).astype(jnp.bfloat16)
    mlp_out = lax.psum_scatter(
        dot_plain(act_low, contract_weight).astype(jnp.bfloat16),
        "fsdp",
        scatter_dimension=0,
        tiled=True,
    ).astype(jnp.float32)
    mlp_out = mlp_out + full_contractbias.astype(jnp.float32)
    block_out = (x_rows + attn_out + mlp_out).astype(jnp.bfloat16).reshape(tokens.shape)
    out_rows = cotangent.reshape(row_count, feat_width)
    out_sum = jnp.sum(out_rows.astype(jnp.float32), axis=0)
    gelu_back = jax.vjp(partial(jax.nn.gelu, approximate=False), pre_act)[1]
    group_grads = lax.all_gather(out_rows, "fsdp", axis=0, tiled=True)
    contract_part = dot_left(act_low, group_grads)
    pre_grad = gelu_back(dot_right(group_grads, contract_weight))[0].astype(jnp.bfloat16)
    expand_part = dot_left(group_rows, pre_grad)
    expandbias_part = jnp.sum(pre_grad.astype(jnp.float32), axis=0)
    mlpin_grad = lax.psum_scatter(
        dot_right(pre_grad, expand_weight), "fsdp", scatter_dimension=0, tiled=True
    )
    mlp_pull = jax.vjp(layer_norm, x_rows, full_mlpgain.astype(jnp.float32), zero_shift)[1]
    mlpx_grad, mlpgain_grad, mlpshift_grad = mlp_pull(mlpin_grad)
    dense_grad = dot_left(context, out_rows)
    context_grad = dot_right(out_rows, full_dense).astype(jnp.bfloat16)
    grad_heads = lax.all_to_all(
        context_grad.reshape(seq_count, local_len, HEADS, HEAD_DIM),
        "seq",
        split_axis=2,
        concat_axis=1,
        tiled=True,
    )
    grad_items = jnp.transpose(grad_heads, (0, 2, 1, 3)).reshape(
        seq_count * head_local, full_len, HEAD_DIM
    )
    query_grad, key_grad, value_grad = lax.map(backward_item, (per_item, grad_items, log_total))
    grads_stacked = jnp.stack([query_grad, key_grad, value_grad], axis=1).astype(jnp.bfloat16)
    grads_stacked = jnp.transpose(
        grads_stacked.reshape(seq_count, head_local, 3, full_len, HEAD_DIM), (0, 3, 2, 1, 4)
    )
    back_tokens = lax.all_to_all(grads_stacked, "seq", split_axis=1, concat_axis=3, tiled=True)
    back_float = back_tokens.astype(jnp.float32)
    rotate_back = jax.vjp(
        partial(rotate, cosine=cosine_table, sine=sine_table), projected[:, :, 0]
    )[1]
    proj_grad = jnp.stack(
        [
            rotate_back(back_float[:, :, 0])[0],
            rotate_back(back_float[:, :, 1])[0],
            back_float[:, :, 2],
        ],
        axis=2,
    )
    proj_grad = proj_grad.astype(jnp.bfloat16).reshape(row_count, 3 * feat_width)
    qkv_grad = dot_left(attn_in, proj_grad)
    qkvbias_grad = jnp.sum(proj_grad.astype(jnp.float32), axis=0)
    attnin_grad = dot_right(proj_grad, full_qkv)
    attn_pull = jax.vjp(layer_norm, x_rows, full_attngain.astype(jnp.float32), zero_shift)[1]
    attnx_grad, attngain_grad, attnshift_grad = attn_pull(attnin_grad)
    (
        qkv_part,
        qkvbias_part,
        dense_part,
        bias_part,
        attngain_part,
        attnshift_part,
        mlpgain_part,
        mlpshift_part,
    ) = (
        lax.psum_scatter(qkv_grad, "fsdp", scatter_dimension=0, tiled=True),
        lax.psum_scatter(qkvbias_grad, "fsdp", scatter_dimension=0, tiled=True),
        lax.psum_scatter(dense_grad, "fsdp", scatter_dimension=0, tiled=True),
        lax.psum_scatter(out_sum, "fsdp", scatter_dimension=0, tiled=True),
        lax.psum_scatter(attngain_grad, "fsdp", scatter_dimension=0, tiled=True),
        lax.psum_scatter(attnshift_grad, "fsdp", scatter_dimension=0, tiled=True),
        lax.psum_scatter(mlpgain_grad, "fsdp", scatter_dimension=0, tiled=True),
        lax.psum_scatter(mlpshift_grad, "fsdp", scatter_dimension=0, tiled=True),
    )
    (
        qkv_total,
        qkvbias_total,
        dense_total,
        bias_total,
        attngain_total,
        attnshift_total,
        mlpgain_total,
        mlpshift_total,
        contract_total,
        expand_total,
        expandbias_total,
    ) = lax.psum(
        (
            qkv_part,
            qkvbias_part,
            dense_part,
            bias_part,
            attngain_part,
            attnshift_part,
            mlpgain_part,
            mlpshift_part,
            contract_part,
            expand_part,
            expandbias_part,
        ),
        "seq",
    )
    input_grad = (out_rows.astype(jnp.float32) + attnx_grad + mlpx_grad).reshape(tokens.shape)
    return (
        block_out,
        input_grad,
        attngain_total,
        attnshift_total,
        mlpgain_total,
        mlpshift_total,
        qkv_total,
        qkvbias_total,
        dense_total,
        bias_total,
        expand_total,
        expandbias_total,
        contract_total,
        bias_total,
    )


def solution(mesh):
    placed = (
        P("fsdp", "seq", None),
        P("fsdp", "seq", None),
        P("fsdp"),
        P("fsdp"),
        P("fsdp"),
        P("fsdp"),
        P("fsdp", None),
        P("fsdp"),
        P("fsdp", None),
        P("fsdp"),
        P(None, "fsdp"),
        P("fsdp"),
        P("fsdp", None),
        P("fsdp"),
    )
    return jax.shard_map(
        shards,
        mesh=mesh,
        in_specs=placed,
        out_specs=(
            P("fsdp", "seq", None),
            P("fsdp", "seq", None),
            P("fsdp"),
            P("fsdp"),
            P("fsdp"),
            P("fsdp"),
            P("fsdp", None),
            P("fsdp"),
            P("fsdp", None),
            P("fsdp"),
            P(None, "fsdp"),
            P("fsdp"),
            P("fsdp", None),
            P("fsdp"),
        ),
        check_vma=False,
    )
```

profile of v0, /device:TPU:0, one launch (start us, length us, event | category | flops | bytes accessed | tf_op | source)
XLA Modules:
  0.0 1960.2 jit_solution(13749775188250407117)
XLA Ops:
  39.2 79.4 %all-gather.17.cloned.1.call-done = bf16[2048,2048]{1,0:T(8,128)(2,1)} async-done(((bf16[256,2048]{1,0:T(8,128)(2,1)}), bf16[2048,2048]{1,0:T(8,128)(2,1)}) %all-gather.17.cloned.1.call-update) | async-done | bytes 8388624 | tf_op jit(solution)/shard_map/all_gather | solution.py:189
  118.7 31.6 %multiply_convert_fusion.2 = (bf16[2048,1024]{1,0:T(8,128)(2,1)}, f32[2048,1024]{1,0:T(8,128)}, f32[2048,1024]{1,0:T(8,128)}) fusion(f32[1024]{0:T(1024)S(1)} %convert_element_type.182, bf16[2048,2048]{1,0:T(8,128)(2,1)} %all-gather.17.cloned.1.call-done, bf16[2048,1024]{1,0:T(8,128)(2,1)} %param.28), kind=kOutput, calls=%fused_computation.73 | convolution fusion | flops 8728346624 | bytes 33558528 | tf_op jit(solution)/shard_map/dot_general | solution.py:44
  150.2 50.7 %all-gather.19.cloned.1.call-done = bf16[1,2048,2048]{2,1,0:T(8,128)(2,1)} async-done(((bf16[1,256,2048]{2,1,0:T(8,128)(2,1)}), bf16[1,2048,2048]{2,1,0:T(8,128)(2,1)}) %all-gather.19.cloned.1.call-update) | async-done | bytes 8388624 | tf_op jit(solution)/shard_map/all_gather | solution.py:203
  200.9 21.8 %convert_reduce_fusion = (f32[1024]{0:T(1024)}, bf16[2048,1024]{1,0:T(8,128)(2,1)S(1)}) fusion(f32[2048,1024]{1,0:T(8,128)} %get-tuple-element.135, bf16[1024,2048]{1,0:T(8,128)(2,1)} %param.30, bf16[1,2048,2048]{2,1,0:T(8,128)(2,1)} %all-gather.19.cloned.1.call-done, f32[2048,1024]{1,0:T(8,128)} %get-tuple-element.170, f32[1024]{0:T(1024)S(1)} %convert_element_type.182), kind=kOutput, calls=%fused_computation.71 | convolution fusion | flops 8625585152 | bytes 33562624 | tf_op jit(solution)/shard_map/dot_general | solution.py:48
  259.8 25.2 %all-gather.3 = bf16[8,1,768]{2,1,0:T(2,128)(2,1)S(1)} all-gather(bf16[1,1,768]{2,1,0:T(2,128)(2,1)S(1)} %reshape.462), channel_id=1, replica_groups=mesh['seq'=4,'fsdp'=8] {'fsdp'}, dimensions={0}, use_global_device_ids=true | all-gather | bytes 13824 | tf_op jit(solution)/shard_map/all_gather | solution.py:151
  285.3 136.0 %all-gather.13.cloned.1.call-done = bf16[2048,6144]{1,0:T(8,128)(2,1)} async-done(((bf16[256,6144]{1,0:T(8,128)(2,1)}), bf16[2048,6144]{1,0:T(8,128)(2,1)}) %all-gather.13.cloned.1.call-update) | async-done | bytes 25165840 | tf_op jit(solution)/shard_map/all_gather | solution.py:150
  453.3 36.6 %all-to-all-done = bf16[1,256,3,8,256]{1,4,2,0,3:T(8,128)(2,1)S(1)} async-done(((bf16[1,256,3,8,256]{1,4,2,0,3:T(8,128)(2,1)}), bf16[1,256,3,8,256]{1,4,2,0,3:T(8,128)(2,1)S(1)}, u32[]{:S(2)}, u32[]{:S(2)}) %all-to-all-start) | async-done | bytes 3145760 | tf_op jit(solution)/shard_map/all_to_all | solution.py:172
  496.3 54.7 %while.26 = (s32[]{:T(128)}, bf16[2,1024,256]{2,0,1:T(2,128)(2,1)}, f32[2,1024]{1,0:T(2,128)S(1)}, bf16[2,3,1024,256]{3,2,1,0:T(8,128)(2,1)S(1)}, s32[]{:T(128)}, /*index=5*/s32[]{:T(128)}, s32[]{}, s32[]{}, s32[]{}) while((s32[]{:T(128)}, bf16[2,1024,256]{2,0,1:T(2,128)(2,1)}, f32[2,1024]{1,0:T(2,128)S(1)}, ...), condition=%wide.region_7.8_spmd, body=%wide.region_2.7_spmd.sunk | while | flops 1084228096 | bytes 18931360 | solution.py:177
  503.3 20.3 %dynamic_update_slice.22 = bf16[2,1024,256]{2,0,1:T(2,128)(2,1)} dynamic-update-slice(bf16[2,1024,256]{2,0,1:T(2,128)(2,1)} %get-tuple-element.278, bf16[1,1024,256]{2,0,1:T(2,128)(2,1)} %copy.95, s32[]{:T(128)S(6)} %copy.107, s32[]{:T(128)} %constant.67.clone.1..sunk, s32[]{:T(128)} %constant.67.clone.1..sunk) | dynamic-update-slice | bytes 1048580 | tf_op jit(solution)/shard_map/while/body/jit(dynamic_update_index_in_dim)/dynamic_update_slice | solution.py:177
  530.7 20.3 %dynamic_update_slice.22 = bf16[2,1024,256]{2,0,1:T(2,128)(2,1)} dynamic-update-slice(bf16[2,1024,256]{2,0,1:T(2,128)(2,1)} %get-tuple-element.278, bf16[1,1024,256]{2,0,1:T(2,128)(2,1)} %copy.95, s32[]{:T(128)S(6)} %copy.107, s32[]{:T(128)} %constant.67.clone.1..sunk, s32[]{:T(128)} %constant.67.clone.1..sunk) | dynamic-update-slice | bytes 1048580 | tf_op jit(solution)/shard_map/while/body/jit(dynamic_update_index_in_dim)/dynamic_update_slice | solution.py:177
  551.0 18.0 all_to_all.60
  613.4 157.9 %while.27 = (s32[]{:T(128)}, bf16[2,1024,256]{2,0,1:T(2,128)(2,1)}, bf16[2,1024,256]{2,0,1:T(2,128)(2,1)}, bf16[2,1024,256]{2,0,1:T(2,128)(2,1)}, bf16[2,3,1024,...) while((s32[]{:T(128)}, bf16[2,1024,256]{2,0,1:T(2,128)(2,1)}, ...), condition=%wide.region_12.13_spmd, body=%wide.region_9.12_spmd.sunk | while | flops 2697723392 | bytes 54033656 | solution.py:225
  625.9 20.3 %dynamic_update_slice.24 = bf16[2,1024,256]{2,0,1:T(2,128)(2,1)} dynamic-update-slice(bf16[2,1024,256]{2,0,1:T(2,128)(2,1)} %get-tuple-element.308, bf16[1,1024,256]{2,0,1:T(2,128)(2,1)} %copy.96, s32[]{:T(128)S(6)} %copy.117, s32[]{:T(128)} %constant.67.clone.1..sunk.1, s32[]{:T(128)} %constant.67.clone.1..sunk.1) | dynamic-update-slice | bytes 1048580 | tf_op jit(solution)/shard_map/while/body/jit(dynamic_update_index_in_dim)/dynamic_update_slice | solution.py:177
  649.0 20.3 %dynamic_update_slice.25 = bf16[2,1024,256]{2,0,1:T(2,128)(2,1)} dynamic-update-slice(bf16[2,1024,256]{2,0,1:T(2,128)(2,1)} %get-tuple-element.309, bf16[1,1024,256]{2,0,1:T(2,128)(2,1)} %copy.97, s32[]{:T(128)S(6)} %copy.117, s32[]{:T(128)} %constant.67.clone.1..sunk.1, s32[]{:T(128)} %constant.67.clone.1..sunk.1) | dynamic-update-slice | bytes 1048580 | tf_op jit(solution)/shard_map/while/body/jit(dynamic_update_index_in_dim)/dynamic_update_slice | solution.py:177
  672.1 20.3 %dynamic_update_slice.26 = bf16[2,1024,256]{2,0,1:T(2,128)(2,1)} dynamic-update-slice(bf16[2,1024,256]{2,0,1:T(2,128)(2,1)} %get-tuple-element.310, bf16[1,1024,256]{2,0,1:T(2,128)(2,1)} %copy.98, s32[]{:T(128)S(6)} %copy.117, s32[]{:T(128)} %constant.67.clone.1..sunk.1, s32[]{:T(128)} %constant.67.clone.1..sunk.1) | dynamic-update-slice | bytes 1048580 | tf_op jit(solution)/shard_map/while/body/jit(dynamic_update_index_in_dim)/dynamic_update_slice | solution.py:177
  704.8 20.3 %dynamic_update_slice.24 = bf16[2,1024,256]{2,0,1:T(2,128)(2,1)} dynamic-update-slice(bf16[2,1024,256]{2,0,1:T(2,128)(2,1)} %get-tuple-element.308, bf16[1,1024,256]{2,0,1:T(2,128)(2,1)} %copy.96, s32[]{:T(128)S(6)} %copy.117, s32[]{:T(128)} %constant.67.clone.1..sunk.1, s32[]{:T(128)} %constant.67.clone.1..sunk.1) | dynamic-update-slice | bytes 1048580 | tf_op jit(solution)/shard_map/while/body/jit(dynamic_update_index_in_dim)/dynamic_update_slice | solution.py:177
  727.9 20.3 %dynamic_update_slice.25 = bf16[2,1024,256]{2,0,1:T(2,128)(2,1)} dynamic-update-slice(bf16[2,1024,256]{2,0,1:T(2,128)(2,1)} %get-tuple-element.309, bf16[1,1024,256]{2,0,1:T(2,128)(2,1)} %copy.97, s32[]{:T(128)S(6)} %copy.117, s32[]{:T(128)} %constant.67.clone.1..sunk.1, s32[]{:T(128)} %constant.67.clone.1..sunk.1) | dynamic-update-slice | bytes 1048580 | tf_op jit(solution)/shard_map/while/body/jit(dynamic_update_index_in_dim)/dynamic_update_slice | solution.py:177
  751.0 20.3 %dynamic_update_slice.26 = bf16[2,1024,256]{2,0,1:T(2,128)(2,1)} dynamic-update-slice(bf16[2,1024,256]{2,0,1:T(2,128)(2,1)} %get-tuple-element.310, bf16[1,1024,256]{2,0,1:T(2,128)(2,1)} %copy.98, s32[]{:T(128)S(6)} %copy.117, s32[]{:T(128)} %constant.67.clone.1..sunk.1, s32[]{:T(128)} %constant.67.clone.1..sunk.1) | dynamic-update-slice | bytes 1048580 | tf_op jit(solution)/shard_map/while/body/jit(dynamic_update_index_in_dim)/dynamic_update_slice | solution.py:177
  777.6 39.7 %all_to_all.61 = bf16[1,1024,3,2,256]{4,3,2,0,1:T(2,128)(2,1)} all-to-all(bf16[1,1024,3,2,256]{4,3,2,0,1:T(2,128)(2,1)S(1)} %maximum_bitcast_fusion.2), channel_id=1, replica_groups=mesh['seq'=4,'fsdp'=8] {'seq'}, dimensions={1} | all-to-all | bytes 6291456 | tf_op jit(solution)/shard_map/all_to_all | solution.py:230
  834.6 21.6 %fusion.70 = f32[2048,6144]{1,0:T(8,128)} fusion(bf16[256,6144]{0,1:T(8,128)(2,1)} %bitcast.315, bf16[1,256,2048]{2,1,0:T(8,128)(2,1)S(1)} %copy-done.1, f32[2048]{0:T(1024)S(1)} %bitcast.337, f32[2048]{0:T(1024)S(1)} %bitcast.332, f32[256]{0:T(256)S(1)} %copy-done.23, f32[256]{0:T(256)S(1)} %copy-done.21), kind=kOutput, calls=%fused_computation.142 | convolution fusion | flops 6445596672 | bytes 54544384 | tf_op jit(solution)/shard_map/dot_general | solution.py:54
  924.5 411.9 %reduce-scatter.9.cloned.1.call-done = f32[256,6144]{1,0:T(8,128)} async-done(((f32[2048,6144]{1,0:T(8,128)}), f32[256,6144]{1,0:T(8,128)}) %reduce-scatter.9.cloned.1.call-update) | async-done | bytes 6291472 | tf_op jit(solution)/shard_map/reduce_scatter | solution.py:259
  1357.9 69.5 %reduce-scatter.5.cloned.1.call-done = bf16[256,2048]{1,0:T(8,128)(2,1)} async-done(((bf16[2048,2048]{1,0:T(8,128)(2,1)}), bf16[256,2048]{1,0:T(8,128)(2,1)}) %reduce-scatter.5.cloned.1.call-update) | async-done | bytes 1048592 | tf_op jit(solution)/shard_map/reduce_scatter | solution.py:192
  1434.5 49.9 %all-reduce.18.cloned.1.call-done = (f32[2048]{0:T(1024)}, f32[2048]{0:T(1024)}, f32[2048]{0:T(1024)}, f32[2048]{0:T(1024)}, f32[6144]{0:T(1024)}, /*index=5*/f32[2048]{0:T(1024)}) async-done(((f32[2048]{0:T(1024)}, f32[2048]{0:T(1024)}, f32[2048]{0:T(1024)}, f32[2048]{0:T(1024)}, f32[6144]{0:T(1024)}, /*index=5*/f32[2048]{0:T(1024)}), (f32[2048]{0:T(1024)}, f32[2048]{0:T(1024)}, f32[2048]{0:T(1024)}, ...) | async-done | bytes 65552
  1506.0 428.9 %all-reduce.20.cloned.1.call-done = (f32[256,6144]{1,0:T(8,128)}, f32[256,2048]{1,0:T(8,128)}, f32[2048,1024]{1,0:T(8,128)}, f32[1024,2048]{1,0:T(8,128)}) async-done(((f32[256,6144]{1,0:T(8,128)}, f32[256,2048]{1,0:T(8,128)}, f32[2048,1024]{1,0:T(8,128)}, f32[1024,2048]{1,0:T(8,128)}), (f32[256,6144]{1,0:T(8,128)}, f32[256,2048]{1,0:T(8,128)}, f32[2048,1024]{1,0:T(8,128)}, ...) | async-done | bytes 25165840 | tf_op jit(solution)/shard_map/psum | solution.py:280
  (255 shorter events, 360.7 us)
Async XLA Ops:
  7.2 111.5 %all-gather.17.cloned.1.call-start = ((), (), s32[]{:S(2)}) async-start(), calls=%async_computation.10 | async-start | bytes 9437184 | tf_op jit(solution)/shard_map/all_gather | solution.py:189
  10.0 411.3 %copy-start.20 = (f32[256]{0:T(256)}, f32[256]{0:T(256)S(1)}, u32[]{:S(2)}) copy-start(f32[256]{0:T(256)S(1)} %broadcast_multiply_fusion) | copy-start | bytes 3076
  12.2 409.0 %copy-start.22 = (f32[256]{0:T(256)}, f32[256]{0:T(256)S(1)}, u32[]{:S(2)}) copy-start(f32[256]{0:T(256)S(1)} %fusion.84) | copy-start | bytes 3076
  37.1 163.8 %all-gather.19.cloned.1.call-start = ((), (), s32[]{:S(2)}) async-start(), calls=%async_computation.15 | async-start | bytes 9437184 | tf_op jit(solution)/shard_map/all_gather | solution.py:203
  37.8 383.4 %all-gather.13.cloned.1.call-start = ((), (), s32[]{:S(2)}) async-start(), calls=%async_computation.8 | async-start | bytes 28311552 | tf_op jit(solution)/shard_map/all_gather | solution.py:150
  38.6 543.4 %all-gather.15.cloned.1.call-start = ((), (), s32[]{:S(2)}) async-start(), calls=%async_computation.9 | async-start | bytes 9437184 | tf_op jit(solution)/shard_map/all_gather | solution.py:152
  39.2 847.0 %reduce-scatter.7.cloned.1.call-start = ((), (), s32[]{:S(2)}) async-start(), calls=%async_computation.12 | async-start | bytes 18874368 | tf_op jit(solution)/shard_map/reduce_scatter | solution.py:208
  200.9 23.7 %copy-start.30 = (bf16[2048,1024]{1,0:T(8,128)(2,1)S(1)}, bf16[2048,1024]{1,0:T(8,128)(2,1)}, u32[]{:S(2)}) copy-start(bf16[2048,1024]{1,0:T(8,128)(2,1)} %param.28) | copy-start | bytes 12582916
  236.4 184.8 %copy-start = (bf16[1,256,2048]{2,1,0:T(8,128)(2,1)S(1)}, bf16[1,256,2048]{2,1,0:T(8,128)(2,1)}, u32[]{:S(2)}) copy-start(bf16[1,256,2048]{2,1,0:T(8,128)(2,1)} %param.18) | copy-start | bytes 3145732
  245.9 189.8 %copy-start.16 = (f32[8,1,256]{2,1,0:T(1,128)}, f32[8,1,256]{2,1,0:T(1,128)S(1)}, u32[]{:S(2)}) copy-start(f32[8,1,256]{2,1,0:T(1,128)S(1)} %convert_element_type.205) | copy-start | bytes 24580
  259.8 175.8 %copy-start.10 = (f32[8,1,256]{2,1,0:T(1,128)}, f32[8,1,256]{2,1,0:T(1,128)S(1)}, u32[]{:S(2)}) copy-start(f32[8,1,256]{2,1,0:T(1,128)S(1)} %convert_element_type.204) | copy-start | bytes 24580
  285.3 161.6 %copy-start.12 = (f32[256,32]{0,1:T(8,128)}, f32[256,32]{0,1:T(8,128)S(1)}, u32[]{:S(2)}) copy-start(f32[256,32]{0,1:T(8,128)S(1)} %get-tuple-element.168) | copy-start | bytes 98308
  285.3 161.6 %copy-start.14 = (f32[256,32]{0,1:T(8,128)}, f32[256,32]{0,1:T(8,128)S(1)}, u32[]{:S(2)}) copy-start(f32[256,32]{0,1:T(8,128)S(1)} %get-tuple-element.169) | copy-start | bytes 98308
  449.5 40.4 %all-to-all-start = ((bf16[1,256,3,8,256]{1,4,2,0,3:T(8,128)(2,1)}), bf16[1,256,3,8,256]{1,4,2,0,3:T(8,128)(2,1)S(1)}, u32[]{:S(2)}, u32[]{:S(2)}) async-start(bf16[1,256,3,8,256]{1,4,2,0,3:T(8,128)(2,1)} %copy.50), calls=%async_computation | async-start | bytes 6291456 | tf_op jit(solution)/shard_map/all_to_all | solution.py:172
  453.2 471.2 %reduce-scatter.11.cloned.1.call-start = ((), (), s32[]{:S(2)}) async-start(), calls=%async_computation.14 | async-start | bytes 18874368 | tf_op jit(solution)/shard_map/reduce_scatter | solution.py:261
  589.8 16.8 all-to-all-start.2
  594.1 742.2 %reduce-scatter.9.cloned.1.call-start = ((), (), s32[]{:S(2)}) async-start(), calls=%async_computation.13 | async-start | bytes 56623104 | tf_op jit(solution)/shard_map/reduce_scatter | solution.py:259
  856.2 571.1 %reduce-scatter.5.cloned.1.call-start = ((), (), s32[]{:S(2)}) async-start(), calls=%async_computation.11 | async-start | bytes 9437184 | tf_op jit(solution)/shard_map/reduce_scatter | solution.py:192
  870.3 15.8 copy-start.19
  870.3 614.1 %all-reduce.18.cloned.1.call-start = ((), (), s32[]{:S(2)}) async-start(), calls=%async_computation.16 | async-start | bytes 131072
  909.5 1025.4 %all-reduce.20.cloned.1.call-start = ((), (), s32[]{:S(2)}) async-start(), calls=%async_computation.17 | async-start | bytes 50331648 | tf_op jit(solution)/shard_map/psum | solution.py:280
  1336.3 91.0 %copy-start.4 = (bf16[1,256,4,2,256]{1,4,3,2,0:T(8,128)(2,1)S(1)}, bf16[1,256,4,2,256]{1,4,3,2,0:T(8,128)(2,1)}, u32[]{:S(2)}) copy-start(bf16[1,256,4,2,256]{1,4,3,2,0:T(8,128)(2,1)} %copy.54) | copy-start | bytes 3145732
  1427.4 61.6 %copy-start.26 = (f32[1024]{0:T(1024)S(1)}, f32[1024]{0:T(1024)}, u32[]{:S(2)}) copy-start(f32[1024]{0:T(1024)} %get-tuple-element.172) | copy-start | bytes 12292
  1505.9 436.2 %copy-start.29 = (f32[256]{0:T(256)}, f32[256]{0:T(256)S(1)}, u32[]{:S(2)}) copy-start(f32[256]{0:T(256)S(1)} %get-tuple-element.368) | copy-start | bytes 3076
  (28 other events, 90.2 us)
Sparse Core Ops, SparseCore 0:
  37.2 81.4 all-gather.16
  120.3 80.5 all-gather.18
  202.5 218.6 all-gather.12
  422.7 80.2 all-gather.14
  505.2 166.8 reduce-scatter.6
  674.3 166.5 reduce-scatter.10
  856.4 479.9 reduce-scatter.8
  1339.3 88.0 reduce-scatter.4
  1431.5 52.8 all-reduce.17
  1488.8 445.9 all-reduce.19
where the time goes:
time: 1990 us; the launch traced here: 1960 us
  waiting for transfers between devices  1280 us (64%)
  local copies, waits for them, and re-layouts  260 us (13%)
  matrix products  206 us (10%)
  blocking collectives  164 us (8%)
  other arithmetic  28.5 us (1%)
    psum x1, waiting for transfers between devices, shards(): lax.psum((qkv_part, qkvbias_part, dense_part, bias_part, attngain_part, a...  429 us
    reduce_scatter x1, waiting for transfers between devices, shards(): lax.psum_scatter(qkv_grad, 'fsdp', scatter_dimension=0, tiled=True)  412 us
    dynamic_update_slice x18, local copies, waits for them, and re-layouts, shards(): attended, log_total = lax.map(forward_item, per_item)  183 us
    all_gather x1, waiting for transfers between devices, shards(): lax.all_gather(qkv_weight, 'fsdp', axis=0, tiled=True)  136 us
    all_gather x1, waiting for transfers between devices, shards(): group_rows = lax.all_gather(mlp_in, 'fsdp', axis=0, tiled=True)  79.4 us
    dot_general x12, matrix products, dot_plain(): return jnp.dot(left, right, preferred_element_type=jnp.float32)  71 us
    reduce_scatter x1, waiting for transfers between devices, shards(): lax.psum_scatter(dot_plain(act_low, contract_weight).astype(jnp.bfloat16)...  69.5 us
    dot_general x12, matrix products, dot_left(): lax.dot_general(left, right, (((0,), (0,)), ((), ())), preferred_element_...  68.5 us
  transfers between devices with their start and end apart: 12, of which 9 were waited for; matrix products, arithmetic and copies ran while one was open for 24% of the time, Pallas kernels for 0%

commit v1 on v0

v1 whole, which is shorter than its diff:
```python
from functools import partial

import jax
import jax.numpy as jnp
from jax import lax
from jax.experimental import pallas as pl
from jax.experimental.pallas import tpu as pltpu
from jax.sharding import PartitionSpec as P

HEADS = 8
HEAD_DIM = 256
ROT = 64
EPSILON = 1e-05
QUERY_BLOCK = 256


def dot_plain(left, right):
    return jnp.dot(left, right, preferred_element_type=jnp.float32)


def dot_right(left, right):
    return lax.dot_general(
        left, right, (((1,), (1,)), ((), ())), preferred_element_type=jnp.float32
    )


def dot_left(left, right):
    return lax.dot_general(
        left, right, (((0,), (0,)), ((), ())), preferred_element_type=jnp.float32
    )


def rotary_tables(length):
    half = ROT // 2
    frequency = 1.0 / 10000.0 ** (jnp.arange(0, ROT, 2, dtype=jnp.float32) / ROT)
    angles = lax.iota(jnp.int32, length).astype(jnp.float32)[:, None] * frequency[None, :]
    cosine, sine = jnp.cos(angles), jnp.sin(angles)
    zero = jnp.zeros((length, half), jnp.float32)
    rest = 128 - ROT
    return (
        jnp.concatenate([cosine, cosine, jnp.ones((length, rest), jnp.float32)], axis=1),
        jnp.concatenate([-sine, zero, jnp.zeros((length, rest), jnp.float32)], axis=1),
        jnp.concatenate([zero, sine, jnp.zeros((length, rest), jnp.float32)], axis=1),
    )


def rotate(rows, cosine, sine_low, sine_high, sign):
    part = rows[:, :128]
    turned = part * cosine + sign * (
        pltpu.roll(part, 128 - ROT // 2, 1) * sine_low + pltpu.roll(part, ROT // 2, 1) * sine_high
    )
    return jnp.concatenate([turned, rows[:, 128:]], axis=1)


def softmax_block(query_block, key_rows):
    size, width = query_block.shape[0], key_rows.shape[0]
    scores = dot_right(query_block, key_rows) * HEAD_DIM ** (-0.5)
    row = lax.broadcasted_iota(jnp.int32, (size, width), 0) + (width - size)
    column = lax.broadcasted_iota(jnp.int32, (size, width), 1)
    scores = jnp.where(row >= column, scores, -jnp.inf)
    exponent = jnp.exp(scores - jnp.max(scores, axis=-1, keepdims=True))
    return exponent / jnp.sum(exponent, axis=-1, keepdims=True)


VMEM_LIMIT = 56 * 1024 * 1024
ROW_BLOCK = 256
UNIT_BLOCK = 256


def params(**more):
    return pltpu.CompilerParams(vmem_limit_bytes=VMEM_LIMIT, **more)


def light():
    return pl.CostEstimate(flops=1024, bytes_accessed=1024, transcendentals=0)


def normal_rows(values):
    center = jnp.mean(values, axis=-1, keepdims=True)
    offset_rows = values - center
    spread = jnp.mean(offset_rows * offset_rows, axis=-1, keepdims=True)
    inverse = lax.rsqrt(spread + EPSILON)
    return offset_rows * inverse, inverse


def qkv_kernel(
    rotated, x_ref, vec_ref, weight_ref, bias_ref, cos_ref, low_ref, high_ref, attn_ref, mlp_ref, out_ref
):
    normal, _ = normal_rows(x_ref[...].astype(jnp.float32))
    attn_in = (normal * vec_ref[0:1, :] + vec_ref[1:2, :]).astype(jnp.bfloat16)
    attn_ref[...] = attn_in
    mlp_ref[...] = (normal * vec_ref[2:3, :] + vec_ref[3:4, :]).astype(jnp.bfloat16)
    for head in range(weight_ref.shape[1] // HEAD_DIM):
        columns = pl.ds(head * HEAD_DIM, HEAD_DIM)
        value = dot_plain(attn_in, weight_ref[:, columns]) + bias_ref[:, columns]
        if head < rotated:
            value = rotate(value, cos_ref[...], low_ref[...], high_ref[...], 1.0)
        out_ref[:, columns] = value.astype(jnp.bfloat16)


def project_heads(x_rows, vectors, weight, bias, tables, local):
    total, width = x_rows.shape
    heads_width = 3 * local * HEAD_DIM
    cycle = tables[0].shape[0] // ROW_BLOCK
    rows = lambda columns: pl.BlockSpec((ROW_BLOCK, columns), lambda i: (i, 0))
    whole = lambda shape: pl.BlockSpec(shape, lambda i: (0, 0))
    table = pl.BlockSpec((ROW_BLOCK, 128), lambda i: (lax.rem(i, cycle), 0))
    return pl.pallas_call(
        partial(qkv_kernel, 2 * local),
        grid=(total // ROW_BLOCK,),
        out_shape=[
            jax.ShapeDtypeStruct((total, width), jnp.bfloat16),
            jax.ShapeDtypeStruct((total, width), jnp.bfloat16),
            jax.ShapeDtypeStruct((total, heads_width), jnp.bfloat16),
        ],
        in_specs=[
            rows(width),
            whole(vectors.shape),
            whole((width, heads_width)),
            whole((1, heads_width)),
            table,
            table,
            table,
        ],
        out_specs=[rows(width), rows(width), rows(heads_width)],
        compiler_params=params(),
        cost_estimate=light(),
    )(x_rows, vectors, weight, bias, *tables)


def attend_kernel(
    local, qkv_ref, cot_ref, dense_ref, cos_ref, low_ref, high_ref, ctx_ref, out_ref, key_acc, value_acc
):
    length = qkv_ref.shape[0]
    score_scale = HEAD_DIM ** (-0.5)
    for head in range(local):
        columns = pl.ds(head * HEAD_DIM, HEAD_DIM)
        key_columns = pl.ds((local + head) * HEAD_DIM, HEAD_DIM)
        value_columns = pl.ds((2 * local + head) * HEAD_DIM, HEAD_DIM)
        key_acc[...] = jnp.zeros_like(key_acc)
        value_acc[...] = jnp.zeros_like(value_acc)
        for start in range(0, length, QUERY_BLOCK):
            stop = start + QUERY_BLOCK
            query_block = qkv_ref[start:stop, columns]
            grad_block = dot_right(cot_ref[start:stop, :], dense_ref[columns, :]).astype(
                jnp.bfloat16
            )
            probs = softmax_block(query_block, qkv_ref[:stop, key_columns])
            probs_low = probs.astype(jnp.bfloat16)
            ctx_ref[start:stop, columns] = dot_plain(
                probs_low, qkv_ref[:stop, value_columns]
            ).astype(jnp.bfloat16)
            value_acc[:stop, :] += dot_left(probs_low, grad_block)
            probs_grad = dot_right(grad_block, qkv_ref[:stop, value_columns])
            inner_sum = jnp.sum(probs * probs_grad, axis=-1, keepdims=True)
            score_grad = (probs * (probs_grad - inner_sum)).astype(jnp.bfloat16)
            key_acc[:stop, :] += dot_left(score_grad, query_block)
            query_grad = dot_plain(score_grad, qkv_ref[:stop, key_columns]) * score_scale
            query_grad = query_grad.astype(jnp.bfloat16).astype(jnp.float32)
            out_ref[start:stop, columns] = rotate(
                query_grad,
                cos_ref[start:stop, :],
                low_ref[start:stop, :],
                high_ref[start:stop, :],
                -1.0,
            ).astype(jnp.bfloat16)
        key_grad = (key_acc[...] * score_scale).astype(jnp.bfloat16).astype(jnp.float32)
        out_ref[:, key_columns] = rotate(
            key_grad, cos_ref[...], low_ref[...], high_ref[...], -1.0
        ).astype(jnp.bfloat16)
        out_ref[:, value_columns] = value_acc[...].astype(jnp.bfloat16)


def attend(qkv, cot_rows, dense_part, tables, local):
    length = qkv.shape[0]
    vmem = pl.BlockSpec(memory_space=pltpu.VMEM)
    return pl.pallas_call(
        partial(attend_kernel, local),
        out_shape=[
            jax.ShapeDtypeStruct((length, local * HEAD_DIM), jnp.bfloat16),
            jax.ShapeDtypeStruct(qkv.shape, jnp.bfloat16),
        ],
        in_specs=[vmem] * 6,
        out_specs=[vmem] * 2,
        scratch_shapes=[pltpu.VMEM((length, HEAD_DIM), jnp.float32)] * 2,
        compiler_params=params(),
        cost_estimate=light(),
    )(qkv, cot_rows, dense_part, *tables)


def up_kernel(mlp_ref, cot_ref, weight_ref, bias_ref, act_ref, slope_ref, grad_ref):
    pre = dot_right(mlp_ref[...], weight_ref[...]) + bias_ref[...]
    below = 0.5 * (1.0 + lax.erf(pre * 0.5**0.5))
    act = (pre * below).astype(jnp.bfloat16)
    act_ref[...] = act
    slope_ref[...] = below + pre * (0.3989422804014327 * jnp.exp(-0.5 * pre * pre))
    grad_ref[...] = dot_left(act, cot_ref[...]).astype(jnp.bfloat16)


def expand_units(mlp_in, cot_rows, weight, bias):
    total, width = mlp_in.shape
    hidden = weight.shape[0]
    whole = pl.BlockSpec((total, width), lambda j: (0, 0))
    units = pl.BlockSpec((UNIT_BLOCK, width), lambda j: (j, 0))
    column = pl.BlockSpec((total, UNIT_BLOCK), lambda j: (0, j))
    return pl.pallas_call(
        up_kernel,
        grid=(hidden // UNIT_BLOCK,),
        out_shape=[
            jax.ShapeDtypeStruct((total, hidden), jnp.bfloat16),
            jax.ShapeDtypeStruct((total, hidden), jnp.float32),
            jax.ShapeDtypeStruct((hidden, width), jnp.bfloat16),
        ],
        in_specs=[whole, whole, units, pl.BlockSpec((1, UNIT_BLOCK), lambda j: (0, j))],
        out_specs=[column, column, units],
        compiler_params=params(),
        cost_estimate=light(),
    )(mlp_in, cot_rows, weight, bias)


def down_kernel(mlp_ref, cot_ref, weight_ref, slope_ref, pre_ref, grad_ref, sum_ref):
    pre_grad = (dot_right(cot_ref[...], weight_ref[...]) * slope_ref[...]).astype(jnp.bfloat16)
    pre_ref[...] = pre_grad
    grad_ref[...] = dot_left(pre_grad, mlp_ref[...]).astype(jnp.bfloat16)
    sum_ref[...] = jnp.sum(pre_grad.astype(jnp.float32), axis=0, keepdims=True)


def contract_units(mlp_in, cot_rows, weight, slope):
    total, width = mlp_in.shape
    hidden = weight.shape[0]
    whole = pl.BlockSpec((total, width), lambda j: (0, 0))
    units = pl.BlockSpec((UNIT_BLOCK, width), lambda j: (j, 0))
    column = pl.BlockSpec((total, UNIT_BLOCK), lambda j: (0, j))
    return pl.pallas_call(
        down_kernel,
        grid=(hidden // UNIT_BLOCK,),
        out_shape=[
            jax.ShapeDtypeStruct((total, hidden), jnp.bfloat16),
            jax.ShapeDtypeStruct((hidden, width), jnp.bfloat16),
            jax.ShapeDtypeStruct((1, hidden), jnp.float32),
        ],
        in_specs=[whole, whole, units, column],
        out_specs=[column, units, pl.BlockSpec((1, UNIT_BLOCK), lambda j: (0, j))],
        compiler_params=params(),
        cost_estimate=light(),
    )(mlp_in, cot_rows, weight, slope)


def norm_kernel(x_ref, proj_ref, pre_ref, vec_ref, qkv_ref, expand_ref, part_ref, sums_ref):
    normal, _ = normal_rows(x_ref[...].astype(jnp.float32))

    @pl.when(pl.program_id(0) == 0)
    def _():
        sums_ref[...] = jnp.zeros_like(sums_ref)

    grad = dot_right(proj_ref[...], qkv_ref[...])
    sums_ref[0:1, :] += jnp.sum(grad * normal, axis=0, keepdims=True)
    sums_ref[1:2, :] += jnp.sum(grad, axis=0, keepdims=True)
    part = grad * vec_ref[0:1, :]
    grad = dot_plain(pre_ref[...], expand_ref[...])
    sums_ref[2:3, :] += jnp.sum(grad * normal, axis=0, keepdims=True)
    sums_ref[3:4, :] += jnp.sum(grad, axis=0, keepdims=True)
    part_ref[...] = (part + grad * vec_ref[2:3, :]).astype(jnp.bfloat16)


def norm_parts(x_rows, proj_grad, pre_grad, vectors, qkv_part, expand_part):
    total, width = x_rows.shape
    rows = lambda columns: pl.BlockSpec((ROW_BLOCK, columns), lambda i: (i, 0))
    whole = lambda shape: pl.BlockSpec(shape, lambda i: (0, 0))
    return pl.pallas_call(
        norm_kernel,
        grid=(total // ROW_BLOCK,),
        out_shape=[
            jax.ShapeDtypeStruct((total, width), jnp.bfloat16),
            jax.ShapeDtypeStruct((8, width), jnp.float32),
        ],
        in_specs=[
            rows(width),
            rows(proj_grad.shape[1]),
            rows(pre_grad.shape[1]),
            whole(vectors.shape),
            whole((width, proj_grad.shape[1])),
            whole(expand_part.shape),
        ],
        out_specs=[rows(width), whole((8, width))],
        compiler_params=params(),
        cost_estimate=light(),
    )(x_rows, proj_grad, pre_grad, vectors, qkv_part, expand_part)


def out_kernel(ctx_ref, act_ref, dense_ref, contract_ref, out_ref):
    total = dot_plain(act_ref[...], contract_ref[...]) + dot_plain(ctx_ref[...], dense_ref[...])
    out_ref[...] = total.astype(jnp.bfloat16)


def out_parts(context, act, dense_part, contract_part):
    total = context.shape[0]
    width = dense_part.shape[1]
    rows = lambda columns: pl.BlockSpec((ROW_BLOCK, columns), lambda i: (i, 0))
    whole = lambda shape: pl.BlockSpec(shape, lambda i: (0, 0))
    return pl.pallas_call(
        out_kernel,
        grid=(total // ROW_BLOCK,),
        out_shape=jax.ShapeDtypeStruct((total, width), jnp.bfloat16),
        in_specs=[
            rows(context.shape[1]),
            rows(act.shape[1]),
            whole(dense_part.shape),
            whole(contract_part.shape),
        ],
        out_specs=rows(width),
        compiler_params=params(),
        cost_estimate=light(),
    )(context, act, dense_part, contract_part)


def square_kernel(layouts, *refs):
    count = len(layouts)
    blocks, gathered = refs[:count], refs[count : 2 * count]
    own_sem, send_x, recv_x, send_y, recv_y, pass_x, land_x, pass_y, land_y = refs[2 * count :]
    place = lax.axis_index("seq")
    over_x = place + 1 - 2 * lax.rem(place, 2)
    over_y = lax.rem(place + 2, 4)
    barrier = pltpu.get_barrier_semaphore()
    for neighbour in (over_x, over_y):
        pl.semaphore_signal(
            barrier, inc=1, device_id={"seq": neighbour}, device_id_type=pl.DeviceIdType.MESH
        )
    pl.semaphore_wait(barrier, 2)

    pieces = []
    for block, into, layout in zip(blocks, gathered, layouts):
        rows, columns = block.shape
        parts = layout if layout else 1
        each = columns // parts
        for part in range(parts):
            pieces.append((block, into, layout, rows, each, part))

    def view(piece, slot, start, size):
        _, into, layout, rows, each, part = piece
        if not layout:
            first = pl.multiple_of(slot * rows + start, 16)
            return into.at[pl.ds(first, size), :]
        first = pl.multiple_of((part * 4 + slot) * each, 128)
        return into.at[pl.ds(start, size), pl.ds(first, each)]

    def send(source, target, chip, send_sem, recv_sem):
        copy = pltpu.make_async_remote_copy(
            src_ref=source,
            dst_ref=target,
            send_sem=send_sem,
            recv_sem=recv_sem,
            device_id={"seq": chip},
            device_id_type=pl.DeviceIdType.MESH,
        )
        copy.start()
        return copy

    own, to_x, to_y, last = [], [], [], []
    for i, piece in enumerate(pieces):
        block, _, _, rows, each, part = piece
        source = block.at[:, pl.ds(part * each, each)]
        target = view(piece, place, 0, rows)
        to_x.append(send(source, target, over_x, send_x.at[i], recv_x.at[i]))
        to_y.append(send(source, target, over_y, send_y.at[i], recv_y.at[i]))
        copy = pltpu.make_async_copy(source, target, own_sem.at[i])
        copy.start()
        own.append(copy)
    for i, piece in enumerate(pieces):
        half = piece[3] // 2
        to_x[i].wait_recv()
        second = view(piece, over_x, half, half)
        last.append(send(second, second, over_y, pass_y.at[i], land_y.at[i]))
        to_y[i].wait_recv()
        first = view(piece, over_y, 0, half)
        last.append(send(first, first, over_x, pass_x.at[i], land_x.at[i]))
    for copy in last:
        copy.wait()
    for i in range(len(pieces)):
        own[i].wait()
        to_x[i].wait_send()
        to_y[i].wait_send()


def gather_square(blocks, layouts, identity):
    if lax.axis_size("seq") != 4:
        results = []
        for block, layout in zip(blocks, layouts):
            if not layout:
                results.append(lax.all_gather(block, "seq", axis=0, tiled=True))
            else:
                cut = block.reshape(block.shape[0], layout, 1, block.shape[1] // layout)
                full = lax.all_gather(cut, "seq", axis=2, tiled=True)
                results.append(full.reshape(block.shape[0], -1))
        return results
    shapes = [
        jax.ShapeDtypeStruct(
            (4 * b.shape[0], b.shape[1]) if not n else (b.shape[0], 4 * b.shape[1]), b.dtype
        )
        for b, n in zip(blocks, layouts)
    ]
    pieces = sum(max(n, 1) for n in layouts)
    return pl.pallas_call(
        partial(square_kernel, layouts),
        out_shape=shapes,
        in_specs=[pl.BlockSpec(memory_space=pl.ANY)] * len(blocks),
        out_specs=[pl.BlockSpec(memory_space=pl.ANY)] * len(blocks),
        scratch_shapes=[pltpu.SemaphoreType.DMA((pieces,))] * 9,
        compiler_params=pltpu.CompilerParams(collective_id=identity, has_side_effects=True),
        cost_estimate=light(),
    )(*blocks)


def after(array, *others):
    return lax.optimization_barrier((array, *others))[0]


def permute(array, axis, pairs):
    return lax.ppermute(array, axis, pairs)


def line_moves(chips):
    owners = 2 * chips
    up = [(i, i + 2) for i in range(owners - 2)]
    down = [(i + 2, i) for i in range(owners - 2)]
    other = [(i, i ^ 1) for i in range(owners)]
    return up, down, other


def add_low(*terms):
    total = terms[0].astype(jnp.float32)
    for term in terms[1:]:
        total = total + term.astype(jnp.float32)
    return total.astype(terms[0].dtype)


def scatter_owners(parts):
    owners, owner = lax.axis_size("fsdp"), lax.axis_index("fsdp")
    chips, chip, core = owners // 2, owner // 2, lax.rem(owner, 2)
    up, down, other = line_moves(chips)
    by_core = parts.reshape(chips, 2, *parts.shape[1:])
    theirs = lax.dynamic_index_in_dim(by_core, 1 - core, 1, False)
    mine = lax.dynamic_index_in_dim(by_core, core, 1, False)
    sums = add_low(mine, permute(theirs, "fsdp", other))

    def block_for(target):
        return lax.dynamic_index_in_dim(sums, jnp.clip(target, 0, chips - 1), 0, False)

    rising = falling = None
    for step in range(chips - 1, 0, -1):
        send_up, send_down = block_for(chip + step), block_for(chip - step)
        if rising is not None:
            send_up, send_down = add_low(send_up, rising), add_low(send_down, falling)
        rising = permute(send_up, "fsdp", up)
        falling = permute(send_down, "fsdp", down)
    return add_low(block_for(chip), rising, falling)


SQUARE_X = [(i, i ^ 1) for i in range(4)]
SQUARE_Y = [(i, i ^ 2) for i in range(4)]


def scatter_square(parts):
    seqs = lax.axis_size("seq")
    if seqs != 4:
        return lax.psum_scatter(parts, "seq", scatter_dimension=0, tiled=True)
    place, rows = lax.axis_index("seq"), parts.shape[0] // seqs
    half = rows // 2

    def part(target, offset, count):
        return lax.dynamic_slice_in_dim(parts, target * rows + offset, count, 0)

    over_x = permute(part(place ^ 3, 0, half), "seq", SQUARE_X)
    over_y = permute(part(place ^ 3, half, half), "seq", SQUARE_Y)
    to_x = jnp.concatenate(
        [part(place ^ 1, 0, half), add_low(part(place ^ 1, half, half), over_y)], axis=0
    )
    to_y = jnp.concatenate(
        [add_low(part(place ^ 2, 0, half), over_x), part(place ^ 2, half, half)], axis=0
    )
    return add_low(
        part(place, 0, rows), permute(to_x, "seq", SQUARE_X), permute(to_y, "seq", SQUARE_Y)
    )


def sum_square(array):
    if lax.axis_size("seq") != 4:
        return lax.psum(array, "seq")
    array = array + permute(array, "seq", SQUARE_X)
    return array + permute(array, "seq", SQUARE_Y)


def shards(
    tokens,
    cotangent,
    attn_gain,
    attn_shift,
    mlp_gain,
    mlp_shift,
    qkv_weight,
    qkv_bias,
    dense_weight,
    dense_bias,
    expand_weight,
    expand_bias,
    contract_weight,
    contract_bias,
):
    seqs, owners = lax.axis_size("seq"), lax.axis_size("fsdp")
    place, owner = lax.axis_index("seq"), lax.axis_index("fsdp")
    seq_count, local_len, width = tokens.shape
    length = local_len * seqs
    rows_local = seq_count * local_len
    local = HEADS // seqs
    head_width = local * HEAD_DIM
    depth = width // owners
    units = expand_weight.shape[1] // seqs
    hidden = units * owners
    bf16, f32 = jnp.bfloat16, jnp.float32

    def by_sequence(array):
        parts = array.reshape(seqs, seq_count, local_len, width)
        return jnp.swapaxes(parts, 0, 1).reshape(seq_count * length, width)

    def scatter_rows(array):
        parts = array.reshape(seq_count, seqs, local_len, width)
        return scatter_square(jnp.swapaxes(parts, 0, 1).reshape(seqs * rows_local, width))

    attn_own = jnp.concatenate(
        [
            lax.dynamic_slice(
                qkv_weight.reshape(depth, 3, width),
                (0, 0, place * head_width),
                (depth, 3, head_width),
            ).reshape(depth, 3 * head_width),
            lax.dynamic_slice(dense_weight, (0, place * head_width), (depth, head_width)),
        ],
        axis=1,
    )
    expand_own = lax.dynamic_slice(expand_weight, (0, place * units), (width, units)).T
    contract_own = lax.dynamic_slice(contract_weight, (place * units, 0), (units, width))
    attn_part = lax.all_gather(attn_own, "fsdp", axis=0, tiled=True)
    expand_part = lax.all_gather(expand_own, "fsdp", axis=0, tiled=True)
    contract_part = lax.all_gather(contract_own, "fsdp", axis=0, tiled=True)
    dense_part = lax.all_to_all(
        attn_part[:, 3 * head_width :], "seq", split_axis=0, concat_axis=1, tiled=True
    )
    small = jnp.concatenate(
        [
            attn_gain,
            attn_shift,
            mlp_gain,
            mlp_shift,
            dense_bias,
            contract_bias,
            qkv_bias,
            lax.dynamic_slice(expand_bias, (place * units,), (units,)),
        ]
    )
    small = lax.all_gather(small, "fsdp", axis=0, tiled=False).astype(f32)
    vectors = jnp.swapaxes(small[:, : 6 * depth].reshape(owners, 6, depth), 0, 1)
    vectors = jnp.concatenate([vectors.reshape(6, width), jnp.zeros((2, width), f32)], axis=0)
    bias_qkv = small[:, 6 * depth : 9 * depth].reshape(3, seqs, head_width)
    bias_qkv = lax.dynamic_index_in_dim(bias_qkv, place, 1, False).reshape(1, 3 * head_width)
    bias_expand = small[:, 9 * depth :].reshape(1, hidden)

    x_own = tokens.reshape(rows_local, width)
    cot_own = cotangent.reshape(rows_local, width)
    x_rows, cot_rows = [
        by_sequence(rows) for rows in gather_square([x_own, cot_own], (0, 0), 0)
    ]

    tables = rotary_tables(length)
    attn_in, mlp_in, qkv = project_heads(x_rows, vectors, attn_part, bias_qkv, tables, local)
    pairs = [
        attend(
            qkv[item * length : (item + 1) * length],
            cot_rows[item * length : (item + 1) * length],
            dense_part,
            tables,
            local,
        )
        for item in range(seq_count)
    ]
    context = jnp.concatenate([pair[0] for pair in pairs], axis=0)
    proj_grad = jnp.concatenate([pair[1] for pair in pairs], axis=0)
    dense_grad = dot_left(context, cot_rows).astype(bf16)
    dense_grad = lax.all_to_all(dense_grad, "seq", split_axis=1, concat_axis=0, tiled=True)
    qkv_grad = dot_left(attn_in, proj_grad).astype(bf16)
    attn_grad = jnp.concatenate([qkv_grad, dense_grad], axis=1)
    attn_total = lax.psum_scatter(attn_grad, "fsdp", scatter_dimension=0, tiled=True)

    act, slope, contract_grad = expand_units(mlp_in, cot_rows, expand_part, bias_expand)
    contract_total = lax.psum_scatter(contract_grad, "fsdp", scatter_dimension=0, tiled=True)
    pre_grad, expand_grad, expandbias_sum = contract_units(mlp_in, cot_rows, contract_part, slope)
    expand_total = lax.psum_scatter(expand_grad, "fsdp", scatter_dimension=0, tiled=True)

    norm_part, gain_sums = norm_parts(x_rows, proj_grad, pre_grad, vectors, attn_part, expand_part)
    norm_grad = scatter_rows(norm_part).astype(f32)
    normal_own, inverse_own = normal_rows(x_own.astype(f32))
    x_grad = inverse_own * (
        norm_grad
        - jnp.mean(norm_grad, axis=-1, keepdims=True)
        - normal_own * jnp.mean(norm_grad * normal_own, axis=-1, keepdims=True)
    )
    input_grad = cot_own.astype(f32) + x_grad

    out_sum = scatter_rows(out_parts(context, act, dense_part, contract_part)).astype(f32)
    block_out = (x_own.astype(f32) + out_sum + (vectors[4] + vectors[5])).astype(bf16)

    attn_total, contract_total = gather_square([attn_total, contract_total], (4, 0), 1)
    (expand_total,) = gather_square([expand_total.T], (1,), 2)
    qkv_total = attn_total[:, : 3 * width]
    dense_total = attn_total[:, 3 * width :]

    expandbias_sum = lax.dynamic_update_slice(
        jnp.zeros((owners, seqs, units), f32),
        expandbias_sum.reshape(owners, 1, units),
        (0, place, 0),
    )
    qkvbias_sum = jnp.sum(proj_grad.astype(f32), axis=0).reshape(3, 1, head_width)
    qkvbias_sum = lax.dynamic_update_slice(
        jnp.zeros((3, seqs, head_width), f32), qkvbias_sum, (0, place, 0)
    )
    cot_sum = jnp.sum(cot_own.astype(f32), axis=0)
    gain_sums = jnp.swapaxes(gain_sums[:4].reshape(4, owners, depth), 0, 1)
    sums = jnp.concatenate(
        [
            gain_sums.reshape(owners, 4 * depth),
            cot_sum.reshape(owners, depth),
            qkvbias_sum.reshape(owners, 3 * depth),
            expandbias_sum.reshape(owners, seqs * units),
        ],
        axis=1,
    )
    mine = sum_square(scatter_owners(sums.reshape(owners, 1, -1)))[0]
    cuts = [mine[i * depth : (i + 1) * depth] for i in range(5)]
    qkvbias_total = mine[5 * depth : 8 * depth]
    expandbias_total = mine[8 * depth :]
    return (
        block_out.reshape(tokens.shape),
        input_grad.reshape(tokens.shape),
        cuts[0],
        cuts[1],
        cuts[2],
        cuts[3],
        qkv_total.astype(f32),
        qkvbias_total,
        dense_total.astype(f32),
        cuts[4],
        expand_total.astype(f32),
        expandbias_total,
        contract_total.astype(f32),
        cuts[4],
    )


def solution(mesh):
    vector, rows = P("fsdp"), P("fsdp", None)
    tokens = P("fsdp", "seq", None)
    return jax.shard_map(
        shards,
        mesh=mesh,
        in_specs=(
            tokens,
            tokens,
            vector,
            vector,
            vector,
            vector,
            rows,
            vector,
            rows,
            vector,
            P(None, "fsdp"),
            vector,
            rows,
            vector,
        ),
        out_specs=(
            tokens,
            tokens,
            vector,
            vector,
            vector,
            vector,
            rows,
            vector,
            rows,
            vector,
            P(None, "fsdp"),
            vector,
            rows,
            vector,
        ),
        check_vma=False,
    )
```

time: 1990 us -> 692 us (0.35); the launches traced: 1960 us -> 687 us
  waiting for transfers between devices: 1280 us -> 158 us
  Pallas kernels: 0 us -> 333 us
  local copies, waits for them, and re-layouts: 260 us -> 41.2 us
  matrix products: 206 us -> 14.6 us
  blocking collectives: 164 us -> 43.8 us
  other arithmetic: 28.5 us -> 51.6 us
  starting transfers between devices: 8.39 us -> 30.4 us
    reduce_scatter x4 -> x3, waiting for transfers between devices: 481 us -> 0.01 us  [the longest x1 0.01 us: shards(): lax.psum_scatter(expand_grad, 'fsdp', scatter_dimension=0, tiled=True)]
    psum x1 -> x0, waiting for transfers between devices: 429 us -> none  [shards(): lax.psum((qkv_part, qkvbias_part, dense_part, bias_part, attngain_part, a...]
    pallas_call x0 -> x9, Pallas kernels: none -> 333 us  [the longest x3 174 us: gather_square(): pl.pallas_call(partial(square_kernel, layouts), out_shape=shapes, in_spec...]
    dynamic_update_slice x18 -> x2, local copies, waits for them, and re-layouts: 183 us -> 0.14 us  [the longest x1 0.08 us: shards(): lax.dynamic_update_slice(jnp.zeros((3, seqs, head_width), f32), qkvbias_s...]
    all_gather x4 -> x3, waiting for transfers between devices: 266 us -> 92.7 us  [the longest x1 52.6 us: shards(): expand_part = lax.all_gather(expand_own, 'fsdp', axis=0, tiled=True)]
    dot_general x28 -> x0, matrix products: 137 us -> none  [the longest x12 71 us: dot_plain(): return jnp.dot(left, right, preferred_element_type=jnp.float32)]
    all_gather x7 -> x1, blocking collectives: 88.9 us -> 14.4 us  [shards(): small = lax.all_gather(small, 'fsdp', axis=0, tiled=False).astype(f32)]
    dot_general x12 -> x2, matrix products: 68.5 us -> 14.6 us  [dot_left(): lax.dot_general(left, right, (((0,), (0,)), ((), ())), preferred_element_...]
  transfers between devices with their start and end apart: 12 -> 24, of which waited for: 9 -> 15; matrix products, arithmetic and copies ran while one was open for 24% -> 10% of each run, Pallas kernels for 0% -> 33%
where the time goes in v1:
time: 692 us; the launch traced here: 687 us
  Pallas kernels  333 us (48%)
  waiting for transfers between devices  158 us (23%)
  other arithmetic  51.6 us (7%)
  blocking collectives  43.8 us (6%)
  local copies, waits for them, and re-layouts  41.2 us (6%)
  starting transfers between devices  30.4 us (4%)
  between operations  14.9 us (2%)
  matrix products  14.6 us (2%)
    pallas_call x3, Pallas kernels, gather_square(): pl.pallas_call(partial(square_kernel, layouts), out_shape=shapes, in_spec...  174 us
    all_gather x1, waiting for transfers between devices, shards(): expand_part = lax.all_gather(expand_own, 'fsdp', axis=0, tiled=True)  52.6 us
    ppermute x17, waiting for transfers between devices, permute(): return lax.ppermute(array, axis, pairs)  51.4 us
    pallas_call x1, Pallas kernels, expand_units(): pl.pallas_call(up_kernel, grid=(hidden // UNIT_BLOCK,), out_shape=[jax.Sh...  42.6 us
    pallas_call x1, Pallas kernels, contract_units(): pl.pallas_call(down_kernel, grid=(hidden // UNIT_BLOCK,), out_shape=[jax....  41.2 us
    all_gather x1, waiting for transfers between devices, shards(): contract_part = lax.all_gather(contract_own, 'fsdp', axis=0, tiled=True)  40.2 us
    all_to_all x1, blocking collectives, shards(): lax.all_to_all(attn_part[:, 3 * head_width:], 'seq', split_axis=0, concat...  29.5 us
    pallas_call x1, Pallas kernels, norm_parts(): pl.pallas_call(norm_kernel, grid=(total // ROW_BLOCK,), out_shape=[jax.Sh...  27.7 us
  transfers between devices with their start and end apart: 24, of which 15 were waited for; matrix products, arithmetic and copies ran while one was open for 10% of the time, Pallas kernels for 33%

profile of v1, /device:TPU:0, one launch (start us, length us, event | category | flops | bytes accessed | tf_op | source)
XLA Modules:
  0.0 687.1 jit_solution(4698725677876667018)
XLA Ops:
  19.9 72.8 %shard_map.245 = (bf16[1024,2048]{1,0:T(8,128)(2,1)}, bf16[1024,2048]{1,0:T(8,128)(2,1)}) custom-call(bf16[256,2048]{1,0:T(8,128)(2,1)} %bitcast.79, bf16[256,2048]{1,0:T(8,128)(2,1)} %bitcast.85), custom_call_target="tpu_custom_call" | custom-call | flops 1024 | bytes 1024 | tf_op jit(solution)/shard_map/pallas_call | solution.py:403
  95.2 14.4 %all-gather.1 = bf16[8,1,2560]{2,1,0:T(2,128)(2,1)S(1)} all-gather(bf16[1,1,2560]{2,1,0:T(2,128)(2,1)S(1)} %reshape.156), channel_id=2, replica_groups=mesh['seq'=4,'fsdp'=8] {'fsdp'}, dimensions={0}, use_global_device_ids=true | all-gather | bytes 46080 | tf_op jit(solution)/shard_map/all_gather | solution.py:560
  116.0 13.8 %shard_map.246 = (bf16[1024,2048]{1,0:T(8,128)(2,1)}, bf16[1024,2048]{1,0:T(8,128)(2,1)}, bf16[1024,1536]{1,0:T(8,128)(2,1)}) custom-call(bf16[1024,2048]{1,0:T(8,128)(2,1)} %get-tuple-element.31.x_ref, f32[8,2048]{1,0:T(8,128)} %concatenate.46.vec_ref, bf16[2048,2048]{1,0:T(8,128)(2,1)} %all-gather.6.cloned.1.call-done.weight_ref.qkv_ref, ...), custom_call_target="tpu_custom_call" | custom-call | flops 1024 | bytes 1024 | tf_op jit(solution)/shard_map/pallas_call | solution.py:108
  129.8 52.6 %all-gather.8.cloned.1.call-done.weight_ref.expand_ref = bf16[2048,2048]{1,0:T(8,128)(2,1)} async-done(((bf16[256,2048]{1,0:T(8,128)(2,1)}), bf16[2048,2048]{1,0:T(8,128)(2,1)}) %all-gather.8.cloned.1.call-update) | async-done | bytes 8388624 | tf_op jit(solution)/shard_map/all_gather | solution.py:543
  182.3 42.6 %shard_map.248 = (bf16[1024,2048]{1,0:T(8,128)(2,1)}, f32[1024,2048]{1,0:T(8,128)}, bf16[2048,2048]{1,0:T(8,128)(2,1)}) custom-call(bf16[1024,2048]{1,0:T(8,128)(2,1)} %get-tuple-element.35.mlp_ref, bf16[1024,2048]{1,0:T(8,128)(2,1)} %get-tuple-element.33.cot_ref, bf16[2048,2048]{1,0:T(8,128)(2,1)} %all-gather.8.cloned.1.call-done.weight_ref.expand_ref, ...), custom_call_target="tpu_custom_call" | custom-call | flops 1024 | bytes 1024 | tf_op jit(solution)/shard_map/pallas_call | solution.py:206
  224.9 40.2 %all-gather.10.cloned.1.call-done.contract_ref.weight_ref = bf16[2048,2048]{1,0:T(8,128)(2,1)} async-done(((bf16[256,2048]{1,0:T(8,128)(2,1)}), bf16[2048,2048]{1,0:T(8,128)(2,1)}) %all-gather.10.cloned.1.call-update) | async-done | bytes 8388624 | tf_op jit(solution)/shard_map/all_gather | solution.py:544
  265.1 41.2 %shard_map.250 = (bf16[1024,2048]{1,0:T(8,128)(2,1)}, bf16[2048,2048]{1,0:T(8,128)(2,1)}, f32[1,2048]{1,0:T(1,128)}) custom-call(bf16[1024,2048]{1,0:T(8,128)(2,1)} %get-tuple-element.35.mlp_ref, bf16[1024,2048]{1,0:T(8,128)(2,1)} %get-tuple-element.33.cot_ref, bf16[2048,2048]{1,0:T(8,128)(2,1)} %all-gather.10.cloned.1.call-done.contract_ref.weight_ref, ...), custom_call_target="tpu_custom_call" | custom-call | flops 1024 | bytes 1024 | tf_op jit(solution)/shard_map/pallas_call | solution.py:234
  306.4 12.3 %copy.60 = bf16[2048,2048]{0,1:T(8,128)(2,1)} copy(bf16[2048,2048]{1,0:T(8,128)(2,1)} %get-tuple-element.46) | data formatting | bytes 16777216 | tf_op jit(solution)/shard_map/pallas_call | solution.py:234
  320.9 29.5 %all_to_all.38 = bf16[4,512,512]{2,1,0:T(8,128)(2,1)S(1)} all-to-all(bf16[4,512,512]{2,1,0:T(8,128)(2,1)S(1)} %bitcast.78), channel_id=1, replica_groups=mesh['seq'=4,'fsdp'=8] {'seq'}, dimensions={0} | all-to-all | bytes 4194304 | tf_op jit(solution)/shard_map/all_to_all | solution.py:545
  352.0 16.5 %shard_map.247 = (bf16[1024,512]{1,0:T(8,128)(2,1)}, bf16[1024,1536]{1,0:T(8,128)(2,1)}) custom-call(bf16[1024,1536]{1,0:T(8,128)(2,1)} %get-tuple-element.32.qkv_ref, bf16[1024,2048]{1,0:T(8,128)(2,1)} %get-tuple-element.33.cot_ref, bf16[512,2048]{1,0:T(8,128)(2,1)} %bitcast.80, f32[1024,128]{1,0:T(8,128)} %maximum_maximum_fusion.cos_ref, ...), custom_call_target="tpu_custom_call" | custom-call | flops 1024 | bytes 1024 | tf_op jit(solution)/shard_map/pallas_call | solution.py:177
  378.8 11.0 %convolution_convert_fusion = bf16[2048,1536]{1,0:T(8,128)(2,1)} fusion(bf16[1024,2048]{1,0:T(8,128)(2,1)} %get-tuple-element.43, bf16[1024,1536]{1,0:T(8,128)(2,1)S(1)} %copy-done.4), kind=kOutput, calls=%fused_computation.1 | convolution fusion | flops 6445596672 | bytes 13631488 | tf_op jit(solution)/shard_map/dot_general | solution.py:28
  389.8 12.8 %all-to-all-done.1 = bf16[512,4,512]{2,0,1:T(8,128)(2,1)} async-done(((bf16[512,4,512]{2,0,1:T(8,128)(2,1)}), bf16[512,4,512]{2,0,1:T(8,128)(2,1)}, u32[]{:S(2)}, u32[]{:S(2)}) %all-to-all-start.1) | async-done | bytes 2097184 | tf_op jit(solution)/shard_map/all_to_all | solution.py:588
  402.6 8.4 %pad_maximum_fusion = bf16[2048,2048]{1,0:T(8,128)(2,1)} fusion(bf16[2048,512]{1,0:T(8,128)(2,1)} %bitcast.30, bf16[2048,1536]{1,0:T(8,128)(2,1)} %convolution_convert_fusion), kind=kLoop, calls=%fused_computation | loop fusion | flops 16777216 | bytes 16777216 | tf_op jit(solution)/shard_map/concatenate | solution.py:590
  412.4 27.7 %shard_map.251 = (bf16[1024,2048]{1,0:T(8,128)(2,1)}, f32[8,2048]{1,0:T(8,128)}) custom-call(bf16[1024,2048]{1,0:T(8,128)(2,1)} %get-tuple-element.31.x_ref, bf16[1024,1536]{1,0:T(8,128)(2,1)} %get-tuple-element.37.proj_ref, bf16[1024,2048]{1,0:T(8,128)(2,1)} %get-tuple-element.39.pre_ref, f32[8,2048]{1,0:T(8,128)} %concatenate.46.vec_ref, ...), custom_call_target="tpu_custom_call" | custom-call | flops 1024 | bytes 1024 | tf_op jit(solution)/shard_map/pallas_call | solution.py:270
  445.2 17.2 %shard_map.249 = bf16[1024,2048]{1,0:T(8,128)(2,1)} custom-call(bf16[1024,512]{1,0:T(8,128)(2,1)} %get-tuple-element.34.ctx_ref, bf16[1024,2048]{1,0:T(8,128)(2,1)} %get-tuple-element.36.act_ref, bf16[512,2048]{1,0:T(8,128)(2,1)} %bitcast.81, bf16[2048,2048]{1,0:T(8,128)(2,1)} %all-gather.10.cloned.1.call-done.contract_ref.weight_ref), custom_call_target="tpu_custom_call" | custom-call | flops 1024 | bytes 1024 | tf_op jit(solution)/shard_map/pallas_call | solution.py:301
  472.0 7.1 %collective-permute-done.2 = bf16[128,2048]{1,0:T(8,128)(2,1)S(1)} collective-permute-done((bf16[128,2048]{1,0:T(8,128)(2,1)S(1)}, bf16[128,2048]{1,0:T(8,128)(2,1)S(1)}, u32[]{:S(2)}, u32[]{:S(2)}) %collective-permute-start.2) | collective-permute-done | bytes 524320 | tf_op jit(solution)/shard_map/ppermute | solution.py:419
  489.2 14.1 %collective-permute-done.7 = bf16[256,2048]{1,0:T(8,128)(2,1)} collective-permute-done((bf16[256,2048]{1,0:T(8,128)(2,1)}, bf16[256,2048]{1,0:T(8,128)(2,1)}, u32[]{:S(2)}, u32[]{:S(2)}) %collective-permute-start.7) | collective-permute-done | bytes 1048608 | tf_op jit(solution)/shard_map/ppermute | solution.py:419
  506.8 14.8 %collective-permute-done.3 = bf16[256,2048]{1,0:T(8,128)(2,1)S(1)} collective-permute-done((bf16[256,2048]{1,0:T(8,128)(2,1)}, bf16[256,2048]{1,0:T(8,128)(2,1)S(1)}, u32[]{:S(2)}, u32[]{:S(2)}) %collective-permute-start.3) | collective-permute-done | bytes 1048608 | tf_op jit(solution)/shard_map/ppermute | solution.py:419
  537.7 5.0 collective-permute-start.11
  544.4 5.2 collective-permute-done.14
  558.9 34.6 %shard_map.253 = bf16[2048,1024]{1,0:T(8,128)(2,1)} custom-call(bf16[2048,256]{1,0:T(8,128)(2,1)} %bitcast.89), custom_call_target="tpu_custom_call" | custom-call | flops 1024 | bytes 1024 | tf_op jit(solution)/shard_map/pallas_call | solution.py:403
  593.5 6.6 convert_element_type.146
  600.1 66.6 %shard_map.252 = (bf16[256,8192]{1,0:T(8,128)(2,1)}, bf16[1024,2048]{1,0:T(8,128)(2,1)}) custom-call(bf16[256,2048]{1,0:T(8,128)(2,1)} %reduce-scatter.4.cloned.1.call-done.refs_0_, bf16[256,2048]{1,0:T(8,128)(2,1)} %reduce-scatter.6.cloned.1.call-done.refs_1_), custom_call_target="tpu_custom_call" | custom-call | flops 1024 | bytes 1024 | tf_op jit(solution)/shard_map/pallas_call | solution.py:403
  669.5 5.5 slice_convert_fusion
  (170 shorter events, 99.8 us)
Async XLA Ops:
  7.2 108.8 %all-gather.6.cloned.1.call-start = ((), (), s32[]{:S(2)}) async-start(), calls=%async_computation.5 | async-start | bytes 9437184 | tf_op jit(solution)/shard_map/all_gather | solution.py:542
  14.6 167.7 %all-gather.8.cloned.1.call-start = ((), (), s32[]{:S(2)}) async-start(), calls=%async_computation.6 | async-start | bytes 9437184 | tf_op jit(solution)/shard_map/all_gather | solution.py:543
  17.4 247.7 %all-gather.10.cloned.1.call-start = ((), (), s32[]{:S(2)}) async-start(), calls=%async_computation.7 | async-start | bytes 9437184 | tf_op jit(solution)/shard_map/all_gather | solution.py:544
  19.8 539.1 %reduce-scatter.8.cloned.1.call-start = ((), (), s32[]{:S(2)}) async-start(), calls=%async_computation.10 | async-start | bytes 9437184 | tf_op jit(solution)/shard_map/reduce_scatter | solution.py:596
  318.7 281.4 %reduce-scatter.6.cloned.1.call-start = ((), (), s32[]{:S(2)}) async-start(), calls=%async_computation.9 | async-start | bytes 9437184 | tf_op jit(solution)/shard_map/reduce_scatter | solution.py:594
  373.5 29.0 %all-to-all-start.1 = ((bf16[512,4,512]{2,0,1:T(8,128)(2,1)}), bf16[512,4,512]{2,0,1:T(8,128)(2,1)}, u32[]{:S(2)}, u32[]{:S(2)}) async-start(bf16[512,4,512]{2,0,1:T(8,128)(2,1)} %bitcast.82), calls=%async_computation.1 | async-start | bytes 4194304 | tf_op jit(solution)/shard_map/all_to_all | solution.py:588
  378.3 221.8 %reduce-scatter.4.cloned.1.call-start = ((), (), s32[]{:S(2)}) async-start(), calls=%async_computation.8 | async-start | bytes 9437184 | tf_op jit(solution)/shard_map/reduce_scatter | solution.py:591
  442.8 23.5 %collective-permute-start.6 = (bf16[128,2048]{1,0:T(8,128)(2,1)}, bf16[128,2048]{1,0:T(8,128)(2,1)S(1)}, u32[]{:S(2)}, u32[]{:S(2)}) collective-permute-start(bf16[128,2048]{1,0:T(8,128)(2,1)} %get-tuple-element.53), channel_id=1, source_target_pairs={{0,8},{8,0},{16,24},{24,16},{1,9},{9,1},{17,25},{25,17},{2,10},{10... | collective-permute-start | bytes 1572872 | tf_op jit(solution)/shard_map/ppermute | solution.py:419
  444.3 22.0 %collective-permute-start.4 = (bf16[128,2048]{1,0:T(8,128)(2,1)}, bf16[128,2048]{1,0:T(8,128)(2,1)S(1)}, u32[]{:S(2)}, u32[]{:S(2)}) collective-permute-start(bf16[128,2048]{1,0:T(8,128)(2,1)} %get-tuple-element.54), channel_id=1, source_target_pairs={{0,16},{8,24},{16,0},{24,8},{1,17},{9,25},{17,1},{25,9},{2,18},{10... | collective-permute-start | bytes 1572872 | tf_op jit(solution)/shard_map/ppermute | solution.py:419
  464.2 14.9 %collective-permute-start.2 = (bf16[128,2048]{1,0:T(8,128)(2,1)S(1)}, bf16[128,2048]{1,0:T(8,128)(2,1)S(1)}, u32[]{:S(2)}, u32[]{:S(2)}) collective-permute-start(bf16[128,2048]{1,0:T(8,128)(2,1)S(1)} %get-tuple-element.59), channel_id=1, source_target_pairs={{0,8},{8,0},{16,24},{24,16},{1,9},{9,1},{17,25},{25,17},{2,10},{10... | collective-permute-start | bytes 1572872 | tf_op jit(solution)/shard_map/ppermute | solution.py:419
  465.8 14.9 %collective-permute-start = (bf16[128,2048]{1,0:T(8,128)(2,1)S(1)}, bf16[128,2048]{1,0:T(8,128)(2,1)S(1)}, u32[]{:S(2)}, u32[]{:S(2)}) collective-permute-start(bf16[128,2048]{1,0:T(8,128)(2,1)S(1)} %get-tuple-element.60), channel_id=1, source_target_pairs={{0,16},{8,24},{16,0},{24,8},{1,17},{9,25},{17,1},{25,9},{2,18},{10... | collective-permute-start | bytes 1572872 | tf_op jit(solution)/shard_map/ppermute | solution.py:419
  468.9 34.4 %collective-permute-start.7 = (bf16[256,2048]{1,0:T(8,128)(2,1)}, bf16[256,2048]{1,0:T(8,128)(2,1)}, u32[]{:S(2)}, u32[]{:S(2)}) collective-permute-start(bf16[256,2048]{1,0:T(8,128)(2,1)} %pad_maximum_fusion.5), channel_id=1, source_target_pairs={{0,16},{8,24},{16,0},{24,8},{1,17},{9,25},{17,1},{25,9},{2,18},{10... | collective-permute-start | bytes 3145736 | tf_op jit(solution)/shard_map/ppermute | solution.py:419
  471.6 31.7 %collective-permute-start.5 = (bf16[256,2048]{1,0:T(8,128)(2,1)}, bf16[256,2048]{1,0:T(8,128)(2,1)}, u32[]{:S(2)}, u32[]{:S(2)}) collective-permute-start(bf16[256,2048]{1,0:T(8,128)(2,1)} %pad_maximum_fusion.4), channel_id=1, source_target_pairs={{0,8},{8,0},{16,24},{24,16},{1,9},{9,1},{17,25},{25,17},{2,10},{10... | collective-permute-start | bytes 3145736 | tf_op jit(solution)/shard_map/ppermute | solution.py:419
  483.3 38.3 %collective-permute-start.3 = (bf16[256,2048]{1,0:T(8,128)(2,1)}, bf16[256,2048]{1,0:T(8,128)(2,1)S(1)}, u32[]{:S(2)}, u32[]{:S(2)}) collective-permute-start(bf16[256,2048]{1,0:T(8,128)(2,1)} %pad_maximum_fusion.3), channel_id=1, source_target_pairs={{0,16},{8,24},{16,0},{24,8},{1,17},{9,25},{17,1},{25,9},{2,18},{10... | collective-permute-start | bytes 3145736 | tf_op jit(solution)/shard_map/ppermute | solution.py:419
  484.9 36.7 %collective-permute-start.1 = (bf16[256,2048]{1,0:T(8,128)(2,1)}, bf16[256,2048]{1,0:T(8,128)(2,1)S(1)}, u32[]{:S(2)}, u32[]{:S(2)}) collective-permute-start(bf16[256,2048]{1,0:T(8,128)(2,1)} %pad_maximum_fusion.2), channel_id=1, source_target_pairs={{0,8},{8,0},{16,24},{24,16},{1,9},{9,1},{17,25},{25,17},{2,10},{10... | collective-permute-start | bytes 3145736 | tf_op jit(solution)/shard_map/ppermute | solution.py:419
  526.1 1.3 collective-permute-start.8
  527.5 2.8 collective-permute-start.9
  528.8 6.1 collective-permute-start.12
  530.3 6.1 collective-permute-start.10
  536.4 6.6 collective-permute-start.13
  537.7 6.6 collective-permute-start.11
  543.1 6.5 collective-permute-start.14
  549.6 3.8 collective-permute-start.15
  553.4 3.8 collective-permute-start.16
  (18 other events, 722.3 us)
Sparse Core Ops, SparseCore 0:
  14.7 84.7 all-gather.5
  101.7 80.5 all-gather.7
  184.5 80.5 all-gather.9
  318.8 88.1 reduce-scatter.7
  409.2 87.9 reduce-scatter.5
  499.9 88.7 reduce-scatter.3
